TPU v7x, 128 devices: a whole 4x4x4 slice. The times are simulated.
128 devices in a mesh: blk: 32 (over x, y, core), uly: 4 (over z).
Axes of the slice: x: 4, y: 4, z: 4, core: 2. Of those that a mesh axis runs over, the one named last changes fastest.
Arguments:
- queries: bfloat16 [16384, 4096], P(('blk', 'uly')), may hold values from -100 to 100
- keys: bfloat16 [16384, 512], P(('blk', 'uly')), may hold values from -6 to 6
- values: bfloat16 [16384, 512], P(('blk', 'uly')), may hold values from -6 to 6
- segments: int32 [16384], P(('blk', 'uly')), may hold values from 0 to 7, never falling along the last dimension, each value on 1 to 8192 neighbouring positions
Outputs:
- attended: bfloat16 [16384, 4096], P(('blk', 'uly'))
Inputs may be any that keep to these rules, and one draw needn't show every extreme that they name: `segments`: document numbers never fall along the sequence; each document holds 1 to 8192 positions.
All inputs are finite; a program needn't handle non-finite values.
Results may differ from a plain program's by a relative error of at most 0.0039.
Values may be sent and summed in bfloat16 or wider, within the bound.
A program may use at most 64 MiB of HBM per device.

v0:
```python
import jax
import jax.numpy as jnp
from jax import lax
from jax.sharding import Mesh
from jax.sharding import PartitionSpec as P

HEAD_SIZE = 128
BLK_ULY = ("blk_0", "blk_1", "blk_2", "uly")
BLK = ("blk_0", "blk_1", "blk_2")


def laid_out(blocks, dim):
    lengths = list(blocks.shape[1:])
    lengths[dim] *= blocks.shape[0]
    return jnp.moveaxis(blocks, 0, dim).reshape(lengths)


def gather_in_order(value, axes, order):
    blocks = value
    for k in order:
        blocks = lax.all_gather(blocks, axes[k])
    done = order[::-1]
    back = [done.index(k) for k in range(len(axes))]
    blocks = blocks.transpose(*back, *range(len(axes), blocks.ndim))
    return blocks.reshape(-1, *value.shape)


def gather_axes(value, axes, order, dim):
    return laid_out(gather_in_order(value, axes, order), dim)


def in_one_piece(arrays, axis, dim, along):
    both = jnp.concatenate(arrays, axis=along)
    result, at, outs = (lax.all_gather(both, axis, axis=dim, tiled=True), 0, [])
    for a in arrays:
        outs.append(lax.slice_in_dim(result, at, at + a.shape[along], axis=along))
        at += a.shape[along]
    return tuple(outs)


def update(state, qblk, qpos, qseg, kblk, vblk, kpos, kseg):
    top, total, accum = state
    scores = jnp.einsum(
        "qgpd,kgd->gpqk", qblk, kblk, preferred_element_type=jnp.float32
    ) * HEAD_SIZE ** (-0.5)
    allowed = (kpos[None, :] <= qpos[:, None]) & (kseg[None, :] == qseg[:, None])
    scores = jnp.where(allowed, scores, -1e30)
    fresh = jnp.maximum(top, jnp.max(scores, axis=-1))
    probs = jnp.where(allowed, jnp.exp(scores - fresh[..., None]), 0.0)
    factor = jnp.exp(top - fresh)
    total = total * factor + jnp.sum(probs, axis=-1)
    summed = jnp.einsum(
        "gpqk,kgd->qgpd", probs.astype(jnp.bfloat16), vblk, preferred_element_type=jnp.float32
    )
    accum = accum * jnp.transpose(factor, (2, 0, 1))[..., None] + summed
    return (fresh, total, accum)


def local(queries, keys, values, segments):
    qlocal, klocal, vlocal = (
        lax.all_to_all(queries, "uly", split_axis=1, concat_axis=0, tiled=True),
        lax.all_to_all(keys, "uly", split_axis=1, concat_axis=0, tiled=True),
        lax.all_to_all(values, "uly", split_axis=1, concat_axis=0, tiled=True),
    )
    everyone = gather_axes(segments, BLK_ULY, (0, 1, 3, 2), 0)
    rows = qlocal.shape[0]
    half = rows // 2
    head_groups = klocal.shape[1] // HEAD_SIZE
    per = qlocal.shape[1] // HEAD_SIZE // head_groups
    myself = lax.axis_index(BLK)
    offsets = jnp.arange(half, dtype=jnp.int32)
    lower_q = qlocal[:half]
    upper_q = qlocal[half:]
    lower_pos = myself * rows + offsets
    upper_pos = myself * rows + half + offsets
    halves = []
    for qpart, qpos in ((lower_q, lower_pos), (upper_q, upper_pos)):
        qseg = lax.dynamic_slice_in_dim(everyone, qpos[0], half, 0)
        halves.append((qpart.reshape(half, head_groups, per, HEAD_SIZE), qpos, qseg))
    start_state = (
        jnp.full((head_groups, per, half), -1e30, jnp.float32),
        jnp.zeros((head_groups, per, half), jnp.float32),
        jnp.zeros((half, head_groups, per, HEAD_SIZE), jnp.float32),
    )
    carry = (start_state, start_state)
    kpiece, vpiece = in_one_piece((klocal, vlocal), BLK, 0, 1)
    count = kpiece.shape[0]
    block = 512
    number = count // block
    kblocks = kpiece.reshape(number, block, head_groups, HEAD_SIZE)
    vblocks = vpiece.reshape(number, block, head_groups, HEAD_SIZE)
    firsts = jnp.arange(number, dtype=jnp.int32) * block

    def visit(state, item):
        kblk, vblk, first = item
        kpos = first + jnp.arange(block, dtype=jnp.int32)
        kseg = lax.dynamic_slice_in_dim(everyone, first, block, 0)
        final_output = []
        for index in range(2):
            qblk, qpos, qseg = halves[index]
            final_output.append(
                lax.cond(
                    first <= qpos[-1],
                    lambda s: update(s, qblk, qpos, qseg, kblk, vblk, kpos, kseg),
                    lambda s: s,
                    state[index],
                )
            )
        return (tuple(final_output), None)

    carry, unused = lax.scan(visit, carry, (kblocks, vblocks, firsts))
    outputs = []
    for state in carry:
        top, total, accum = state
        normed = accum / jnp.transpose(total, (2, 0, 1))[..., None]
        outputs.append(normed.reshape(half, head_groups * per * HEAD_SIZE).astype(jnp.bfloat16))
    lower_out, upper_out = outputs
    joined = jnp.concatenate([lower_out, upper_out], axis=0)
    return lax.all_to_all(joined, "uly", split_axis=0, concat_axis=1, tiled=True)


def solution(mesh):
    split = Mesh(
        mesh.devices.reshape(4, 4, 2, mesh.shape["uly"]), ("blk_0", "blk_1", "blk_2", "uly")
    )
    return jax.shard_map(
        local,
        mesh=split,
        in_specs=(P(BLK_ULY, None), P(BLK_ULY, None), P(BLK_ULY, None), P(BLK_ULY)),
        out_specs=P(BLK_ULY, None),
        check_vma=False,
    )
```

profile of v0, /device:TPU:31, one launch (start us, length us, event | category | flops | bytes accessed | tf_op | source)
XLA Modules:
  0.0 605.2 jit_solution(18044966402891131127)
XLA Ops:
  8.4 5.0 all-to-all-start
  18.2 7.2 %all_to_all.73 = bf16[128,4,128]{2,0,1:T(8,128)(2,1)S(1)} all-to-all(bf16[128,4,128]{2,0,1:T(8,128)(2,1)S(1)} %copy.49), channel_id=1, replica_groups=mesh['blk_0'=4,'blk_1'=4,'blk_2'=2,'uly'=4] {'uly'}, dimensions={1} | all-to-all | bytes 262144 | tf_op jit(solution)/shard_map/all_to_all | solution.py:63
  35.8 5.3 all-gather.4
  41.1 8.1 %all-gather.5 = s32[4,4,128]{2,1,0:T(4,128)S(1)} all-gather(s32[1,4,128]{2,1,0:T(4,128)S(1)} %bitcast.205), channel_id=3, replica_groups=mesh['blk_0'=4,'blk_1'=4,'blk_2'=2,'uly'=4] {'blk_1'}, dimensions={0}, use_global_device_ids=true | all-gather | bytes 10240 | tf_op jit(solution)/shard_map/all_gather | solution.py:21
  49.2 9.6 %all-gather.2 = s32[16,4,128]{2,1,0:T(4,128)S(1)} all-gather(s32[4,4,128]{2,1,0:T(4,128)S(1)} %all-gather.5), channel_id=4, replica_groups=mesh['blk_0'=4,'blk_1'=4,'blk_2'=2,'uly'=4] {'uly'}, dimensions={0}, use_global_device_ids=true | all-gather | bytes 40960 | tf_op jit(solution)/shard_map/all_gather | solution.py:21
  58.7 11.4 %all-gather.3 = s32[8,4,4,128]{3,2,1,0:T(4,128)S(1)} all-gather(s32[4,4,4,128]{3,2,1,0:T(4,128)S(1)} %bitcast.202), channel_id=5, replica_groups=mesh['blk_0'=4,'blk_1'=4,'blk_2'=2,'uly'=4] {'blk_2'}, dimensions={0}, use_global_device_ids=true | all-gather | bytes 98304 | tf_op jit(solution)/shard_map/all_gather | solution.py:21
  72.0 7.4 %all-gather.8.cloned.1.call-done = bf16[16384,256]{1,0:T(8,128)(2,1)} async-done(((bf16[512,256]{1,0:T(8,128)(2,1)}), bf16[16384,256]{1,0:T(8,128)(2,1)}) %all-gather.8.cloned.1.call-update) | async-done | bytes 8388624 | tf_op jit(solution)/shard_map/all_gather | solution.py:34
  79.4 5.7 fusion.42
  85.3 493.7 %while.20 = (s32[]{:T(128)}, f32[1,8,256]{2,1,0:T(8,128)S(1)}, f32[1,8,256]{2,1,0:T(8,128)S(1)}, f32[256,1,8,128]{3,0,2,1:T(8,128)S(1)}, f32[1,8,256]{2,1,0:T(8,...) while((s32[]{:T(128)}, f32[1,8,256]{2,1,0:T(8,128)S(1)}, ...), condition=%wide.region_9.10_spmd, body=%wide.region_0.9_spmd.sunk | while | flops 1102852608 | bytes 32786988 | solution.py:111
  91.4 3.7 conditional.5
  97.0 3.7 conditional.4
  122.3 3.7 conditional.5
  127.9 3.7 conditional.4
  143.3 3.7 conditional.4
  153.2 3.7 conditional.5
  168.6 3.7 conditional.5
  174.2 3.7 conditional.4
  199.4 3.7 conditional.5
  205.0 3.7 conditional.4
  230.3 3.7 conditional.5
  235.9 3.7 conditional.4
  245.7 3.7 conditional.5
  251.3 3.7 conditional.4
  276.6 3.7 conditional.5
  282.1 3.7 conditional.4
  307.4 3.7 conditional.5
  313.0 3.7 conditional.4
  328.4 3.7 conditional.4
  338.3 3.7 conditional.5
  353.7 3.7 conditional.5
  359.3 3.7 conditional.4
  384.6 3.7 conditional.5
  390.1 3.7 conditional.4
  415.4 3.7 conditional.5
  421.0 3.7 conditional.4
  436.4 3.7 conditional.4
  446.3 3.7 conditional.5
  461.7 3.7 conditional.5
  467.3 3.7 conditional.4
  492.6 3.7 conditional.5
  498.1 3.7 conditional.4
  523.4 3.7 conditional.5
  529.0 3.7 conditional.4
  538.8 3.7 conditional.5
  544.4 3.7 conditional.4
  569.7 3.7 conditional.5
  575.3 3.7 conditional.4
  582.7 13.7 %all_to_all.74 = bf16[4,128,1024]{2,1,0:T(8,128)(2,1)S(1)} all-to-all(bf16[4,128,1024]{2,1,0:T(8,128)(2,1)S(1)} %bitcast.181), channel_id=1, replica_groups=mesh['blk_0'=4,'blk_1'=4,'blk_2'=2,'uly'=4] {'uly'}, dimensions={0} | all-to-all | bytes 2097152 | tf_op jit(solution)/shard_map/all_to_all | solution.py:119
  (704 shorter events, 459.5 us)
Async XLA Ops:
  6.5 29.3 %copy-start = (s32[128]{0:T(128)S(1)}, s32[128]{0:T(128)}, u32[]{:S(2)}) copy-start(s32[128]{0:T(128)} %param.13) | copy-start | bytes 1540
  8.4 9.9 %all-to-all-start = ((bf16[128,4,128]{2,0,1:T(8,128)(2,1)}), bf16[128,4,128]{2,0,1:T(8,128)(2,1)S(1)}, u32[]{:S(2)}, u32[]{:S(2)}) async-start(bf16[128,4,128]{2,0,1:T(8,128)(2,1)} %copy.47), calls=%async_computation | async-start | bytes 262144 | tf_op jit(solution)/shard_map/all_to_all | solution.py:62
  13.4 66.0 %all-gather.8.cloned.1.call-start = ((), (), s32[]{:S(2)}) async-start(), calls=%async_computation.4 | async-start | bytes 8650752 | tf_op jit(solution)/shard_map/all_gather | solution.py:34
  28.5 43.1 %all-to-all-start.2 = ((bf16[128,4,1024]{2,0,1:T(8,128)(2,1)}), bf16[128,4,1024]{2,0,1:T(8,128)(2,1)S(1)}, u32[]{:S(2)}, u32[]{:S(2)}) async-start(bf16[128,4,1024]{2,0,1:T(8,128)(2,1)} %bitcast.169), calls=%async_computation.2 | async-start | bytes 2097152 | tf_op jit(solution)/shard_map/all_to_all | solution.py:61
Sparse Core Ops, SparseCore 0:
  26.3 53.0 all-gather.7
where the time goes:
time: 609 us; the launch traced here: 605 us
  matrix products  152 us (25%)
  loops' own time  150 us (25%)
  local copies, waits for them, and re-layouts  109 us (18%)
  other arithmetic  102 us (17%)
  blocking collectives  55.1 us (9%)
  between operations  17.6 us (3%)
  waiting for transfers between devices  11.1 us (2%)
  starting transfers between devices  8.55 us (1%)
    another operation x1, loops' own time, local(): carry, unused = lax.scan(visit, carry, (kblocks, vblocks, firsts))  146 us
    dot_general x64, matrix products, update(): jnp.einsum('gpqk,kgd->qgpd', probs.astype(jnp.bfloat16), vblk, preferred_...  102 us
    reduce_sum x64, other arithmetic, update(): total = total * factor + jnp.sum(probs, axis=-1)  64.5 us
    dot_general x64, matrix products, update(): jnp.einsum('qgpd,kgd->gpqk', qblk, kblk, preferred_element_type=jnp.float32)  50.2 us
    slice x64, local copies, waits for them, and re-layouts, visit(): qpos[-1]  38.7 us
    all_gather x4, blocking collectives, gather_in_order(): blocks = lax.all_gather(blocks, axes[k])  34.2 us
    squeeze x32, local copies, waits for them, and re-layouts, local(): carry, unused = lax.scan(visit, carry, (kblocks, vblocks, firsts))  31.8 us
    add x32, other arithmetic, visit(): kpos = first + jnp.arange(block, dtype=jnp.int32)  20.7 us
  transfers between devices with their start and end apart: 3, of which 2 were waited for; matrix products, arithmetic and copies ran while one was open for 1% of the time, Pallas kernels for 0%

commit v1 on v0

v1 whole, which is shorter than its diff:
```python
import functools
import jax, jax.numpy as jnp
from jax import lax
from jax.experimental import pallas as pl
from jax.experimental.pallas import tpu as pltpu
from jax.sharding import Mesh
from jax.sharding import PartitionSpec as P

HEAD_SIZE = 128
NDOC = 8
GROUP = 8
SCALE2 = 1.4426950408889634 * HEAD_SIZE ** -0.5
ONES = 16
UNIT = 512
BIG = 2048


def doc_start(info, pos):
    low = jnp.zeros_like(pos)
    for d in range(1, NDOC):
        low = jnp.where(info[d] <= pos, jnp.maximum(low, info[d]), low)
    return low


def contract(a, b, da, db):
    return lax.dot_general(a, b, (((da,), (db,)), ((), ())), preferred_element_type=jnp.float32)


def attend(info, q_ref, k_hbm, v_hbm, o_ref, kbuf, vbuf, qcat, acc, top, sems):
    D = HEAD_SIZE
    tiles, pieces, piece, _ = q_ref.shape
    rows = pieces * piece
    M = GROUP * rows
    part = kbuf.shape[0] // tiles
    shard = UNIT // pieces

    def loads(t):
        at = pl.ds(t * part, part)
        return (
            pltpu.make_async_copy(k_hbm.at[at], kbuf.at[at], sems.at[0, t]),
            pltpu.make_async_copy(v_hbm.at[at], vbuf.at[at], sems.at[1, t]),
        )

    for t in range(tiles):
        for c in loads(t):
            c.start()

    @pl.loop(0, tiles)
    def _(t):
        base = info[NDOC] + t * part
        first = base + info[NDOC + 1]
        last = first + (pieces - 1) * shard + piece - 1
        for c in loads(t):
            c.wait()
        low = doc_start(info, first) // UNIT
        diag = base // UNIT
        lane = lax.broadcasted_iota(jnp.int32, (1, rows), 1)
        qpos = first + (lane // piece) * shard + lane % piece
        qlow = doc_start(info, qpos)

        for g in range(GROUP):
            q = q_ref[t, :, :, g * D:(g + 1) * D].reshape(rows, D).astype(jnp.float32) * SCALE2
            high = q.astype(jnp.bfloat16)
            at = slice(g * rows, (g + 1) * rows)
            qcat[at, :D] = high
            qcat[at, D:] = (q - high.astype(jnp.float32)).astype(jnp.bfloat16)
        acc[...] = jnp.zeros_like(acc)

        def allowed(at, size):
            kpos = at + lax.broadcasted_iota(jnp.int32, (size, rows), 0)
            return (kpos <= qpos) & (kpos >= qlow)

        def masked(p, m):
            return jnp.concatenate(
                [jnp.where(m, p[:, g * rows:(g + 1) * rows], 0.0) for g in range(p.shape[1] // rows)], axis=1)

        def step(at, size):
            at = pl.multiple_of(at, UNIT)
            k = kbuf[pl.ds(at, size), :]
            v = vbuf[pl.ds(at, size), :]
            kk = jnp.concatenate([k, k], axis=1)
            vv = jnp.concatenate([v, jnp.ones((size, ONES), v.dtype)], axis=1)
            p = masked(jnp.exp2(contract(kk, qcat[...], 1, 1)), allowed(at, size))
            acc[...] += contract(vv, p.astype(jnp.bfloat16), 0, 0)

        end = (diag + 1) * UNIT
        units = diag + 1 - low
        per = BIG // UNIT
        big = units // per
        begin = low * UNIT

        @pl.loop(0, big)
        def _(n):
            step(begin + n * BIG, BIG)

        size = BIG // 2
        done = big * BIG
        while size >= UNIT:
            some = (units // (size // UNIT)) % 2

            @pl.when(some == 1)
            def _(done=done, size=size):
                step(begin + done, size)

            done = done + some * size
            size //= 2

        total = acc[D:D + 8, :]
        good = jnp.min(jnp.where((total > 2.0 ** -60) & (total < 2.0 ** 118), 1.0, 0.0))

        @pl.when(good < 0.5)
        def _():
            top[...] = jnp.full_like(top, -1e30)
            acc[...] = jnp.zeros_like(acc)

            def scores(n, g):
                at = pl.multiple_of(n * UNIT, UNIT)
                q = q_ref[t, :, :, pl.ds(pl.multiple_of(g * D, D), D)].reshape(rows, D)
                m = allowed(at, UNIT)
                return jnp.where(m, contract(kbuf[pl.ds(at, UNIT), :], q, 1, 1) * SCALE2, -1e30), m

            @pl.loop(low, diag + 1)
            def _(n):
                @pl.loop(0, GROUP)
                def _(g):
                    at = pl.ds(pl.multiple_of(g * rows, rows), rows)
                    s, _ = scores(n, g)
                    top[:, at] = jnp.maximum(top[:, at], jnp.max(s, axis=0, keepdims=True))

            @pl.loop(low, diag + 1)
            def _(n):
                v = vbuf[pl.ds(pl.multiple_of(n * UNIT, UNIT), UNIT), :]
                vv = jnp.concatenate([v, jnp.ones((UNIT, ONES), v.dtype)], axis=1)

                @pl.loop(0, GROUP)
                def _(g):
                    at = pl.ds(pl.multiple_of(g * rows, rows), rows)
                    s, m = scores(n, g)
                    p = jnp.where(m, jnp.exp2(s - top[:1, at]), 0.0)
                    acc[:, at] += contract(vv, p.astype(jnp.bfloat16), 0, 0)

        for g in range(GROUP):
            at = slice(g * rows, (g + 1) * rows)
            out = acc[:D, at] / acc[D:D + 1, at]
            o_ref[t, :, :, g * D:(g + 1) * D] = out.T.astype(jnp.bfloat16).reshape(pieces, piece, D)


def attention(info, q, k, v):
    tiles, pieces, piece, width = q.shape
    M = GROUP * pieces * piece
    vm = pl.BlockSpec(memory_space=pltpu.VMEM)
    anywhere = pl.BlockSpec(memory_space=pl.ANY)
    return pl.pallas_call(
        attend,
        out_shape=jax.ShapeDtypeStruct(q.shape, jnp.bfloat16),
        in_specs=[pl.BlockSpec(memory_space=pltpu.SMEM), vm, anywhere, anywhere],
        out_specs=vm,
        scratch_shapes=[
            pltpu.VMEM(k.shape, jnp.bfloat16),
            pltpu.VMEM(v.shape, jnp.bfloat16),
            pltpu.VMEM((M, 2 * HEAD_SIZE), jnp.bfloat16),
            pltpu.VMEM((HEAD_SIZE + ONES, M), jnp.float32),
            pltpu.VMEM((8, M), jnp.float32),
            pltpu.SemaphoreType.DMA((2, tiles)),
        ],
        compiler_params=pltpu.CompilerParams(vmem_limit_bytes=56 << 20),
        name="attend",
    )(info, q, k, v)


BLK_ULY = ("blk_0", "blk_1", "blk_2", "uly")
BLK = ("blk_0", "blk_1", "blk_2")


def local(queries, keys, values, segments):
    heads = lax.axis_size("uly")
    columns = lax.axis_size("blk_0")
    rows = queries.shape[0]
    piece = rows // columns
    width = queries.shape[1] // heads
    counts = jnp.sum((segments[None, :] < jnp.arange(NDOC, dtype=jnp.int32)[:, None]).astype(jnp.int32), axis=1)
    starts = lax.psum(counts, BLK_ULY)
    place = lax.axis_index(("blk_1", "blk_2")) * UNIT
    info = jnp.concatenate([starts, jnp.stack([place, lax.axis_index("blk_0") * piece]).astype(jnp.int32)])
    q = queries.reshape(columns, piece, heads, width)
    q = lax.all_to_all(q, "uly", split_axis=2, concat_axis=1, tiled=True)
    q = q.reshape(columns, heads, piece, width)
    q = lax.all_to_all(q, "blk_0", split_axis=0, concat_axis=0, tiled=True)
    kv = jnp.stack([keys, values])
    kv = lax.all_to_all(kv, "uly", split_axis=2, concat_axis=1, tiled=True)
    kv = lax.all_gather(kv, BLK, axis=1, tiled=True)
    out = attention(info, q, kv[0], kv[1])
    out = lax.all_to_all(out, "blk_0", split_axis=0, concat_axis=0, tiled=True)
    out = lax.all_to_all(out, "uly", split_axis=1, concat_axis=3, tiled=True)
    return out.reshape(rows, heads * width)


def solution(mesh):
    split = Mesh(mesh.devices.reshape(4, 4, 2, mesh.shape["uly"]), BLK_ULY)
    return jax.shard_map(
        local,
        mesh=split,
        in_specs=(P(BLK_ULY, None), P(BLK_ULY, None), P(BLK_ULY, None), P(BLK_ULY)),
        out_specs=P(BLK_ULY, None),
        check_vma=False,
    )
```

time: 609 us -> 326 us (0.54)
  Pallas kernels: 0 us -> 165 us
  matrix products: 152 us -> 0 us
  loops' own time: 150 us -> 0 us
  other arithmetic: 102 us -> 1.72 us
  local copies, waits for them, and re-layouts: 109 us -> 14.1 us
  blocking collectives: 55.1 us -> 112 us
    pallas_call x0 -> x1, Pallas kernels: none -> 165 us  [attention(): pl.pallas_call(attend, out_shape=jax.ShapeDtypeStruct(q.shape, jnp.bfloat...]
    dot_general x128 -> x0, matrix products: 152 us -> none  [the longest x64 102 us: update(): jnp.einsum('gpqk,kgd->qgpd', probs.astype(jnp.bfloat16), vblk, preferred_...]
    another operation x65 -> x0, loops' own time: 150 us -> none  [the longest x1 146 us: local(): carry, unused = lax.scan(visit, carry, (kblocks, vblocks, firsts))]
    psum x0 -> x1, blocking collectives: none -> 68.3 us  [local(): starts = lax.psum(counts, BLK_ULY)]
    reduce_sum x64 -> x1, other arithmetic: 64.5 us -> 0.11 us  [local(): jnp.sum((segments[None, :] < jnp.arange(NDOC, dtype=jnp.int32)[:, None])....]
    slice x68 -> x0, local copies, waits for them, and re-layouts: 45.6 us -> none  [the longest x64 38.7 us: visit(): qpos[-1]]
    all_gather x4 -> x0, blocking collectives: 34.2 us -> none  [gather_in_order(): blocks = lax.all_gather(blocks, axes[k])]
    squeeze x32 -> x1, local copies, waits for them, and re-layouts: 31.8 us -> 5.68 us  [local(): out = attention(info, q, kv[0], kv[1])]
  transfers between devices with their start and end apart: 3 -> 3, of which waited for: 2 -> 1; matrix products, arithmetic and copies ran while one was open for 1% -> 3% of each run, Pallas kernels for 0% -> 0%
where the time goes in v1:
time: 326 us; the launch traced here: 322 us
  Pallas kernels  165 us (51%)
  blocking collectives  112 us (34%)
  local copies, waits for them, and re-layouts  14.1 us (4%)
  between operations  13.5 us (4%)
  starting transfers between devices  9.09 us (3%)
  waiting for transfers between devices  6.74 us (2%)
    pallas_call x1, Pallas kernels, attention(): pl.pallas_call(attend, out_shape=jax.ShapeDtypeStruct(q.shape, jnp.bfloat...  165 us
    psum x1, blocking collectives, local(): starts = lax.psum(counts, BLK_ULY)  68.3 us
    all_to_all x1, blocking collectives, local(): out = lax.all_to_all(out, 'uly', split_axis=1, concat_axis=3, tiled=True)  17.3 us
    all_to_all x1, blocking collectives, local(): out = lax.all_to_all(out, 'blk_0', split_axis=0, concat_axis=0, tiled=True)  16.2 us
    all_to_all x1, blocking collectives, local(): kv = lax.all_to_all(kv, 'uly', split_axis=2, concat_axis=1, tiled=True)  10.4 us
    all_to_all x1, waiting for transfers between devices, local(): q = lax.all_to_all(q, 'blk_0', split_axis=0, concat_axis=0, tiled=True)  6.72 us
  transfers between devices with their start and end apart: 3, of which 1 were waited for; matrix products, arithmetic and copies ran while one was open for 3% of the time, Pallas kernels for 0%

profile of v1, /device:TPU:31, one launch (start us, length us, event | category | flops | bytes accessed | tf_op | source)
XLA Modules:
  0.0 322.2 jit_solution(10639214071064820174)
XLA Ops:
  6.5 0.0 all-gather.2.cloned.1.call-start
  6.5 1.0 pad_maximum_fusion
  7.5 0.0 copy-start.1
  7.5 0.2 copy.24
  7.7 10.4 %all_to_all.58 = bf16[2,128,512]{1,0,2:T(2,128)(2,1)S(1)} all-to-all(bf16[2,128,512]{1,0,2:T(2,128)(2,1)S(1)} %copy.24), channel_id=1, replica_groups=mesh['blk_0'=4,'blk_1'=4,'blk_2'=2,'uly'=4] {'uly'}, dimensions={2} | all-to-all | bytes 524288 | tf_op jit(solution)/shard_map/all_to_all | solution.py:190
  18.1 0.9 copy.25
  19.0 0.0 all-gather.2.cloned.1.call-update
  19.0 1.9 reshape.12
  20.9 1.3 copy.22
  22.2 3.5 %all-to-all-start = ((bf16[4,32,4,1024]{3,1,0,2:T(8,128)(2,1)}), bf16[4,32,4,1024]{3,1,0,2:T(8,128)(2,1)S(1)}, u32[]{:S(2)}, u32[]{:S(2)}) async-start(bf16[4,32,4,1024]{3,1,0,2:T(8,128)(2,1)} %copy.22), calls=%async_computation | async-start | bytes 2097152 | tf_op jit(solution)/shard_map/all_to_all | solution.py:186
  25.7 0.0 copy-done.1
  25.7 0.1 convert_reduce_fusion
  25.8 68.3 %psum.7 = s32[8]{0:T(128)S(1)} all-reduce(s32[8]{0:T(128)S(1)} %convert_reduce_fusion), channel_id=1, replica_groups=mesh['blk_0'=4,'blk_1'=4,'blk_2'=2,'uly'=4] {'blk_0','blk_1','blk_2','uly'}, use_global_device_ids=true, to_apply=%region_1.0 | all-reduce | flops 8 | bytes 64 | tf_op jit(solution)/shard_map/psum | solution.py:182
  94.1 0.6 pad_add_fusion.info
  94.7 0.0 all-to-all-done
  94.7 1.1 copy.30
  95.8 5.6 %all-to-all-start.1 = ((bf16[4,4,32,1024]{3,2,1,0:T(8,128)(2,1)}), bf16[4,4,32,1024]{3,2,1,0:T(8,128)(2,1)S(1)}, u32[]{:S(2)}, u32[]{:S(2)}) async-start(bf16[4,4,32,1024]{3,2,1,0:T(8,128)(2,1)} %bitcast.25), calls=%async_computation.1 | async-start | bytes 2097152 | tf_op jit(solution)/shard_map/all_to_all | solution.py:188
  101.4 0.0 all-gather.2.cloned.1.call-done
  101.4 5.7 %slice_bitcast_fusion = (bf16[16384,128]{1,0:T(8,128)(2,1)}, bf16[16384,128]{1,0:T(8,128)(2,1)}) fusion(bf16[2,16384,128]{2,1,0:T(8,128)(2,1)} %all-gather.2.cloned.1.call-done), kind=kLoop, calls=%fused_computation | loop fusion | bytes 16777216 | tf_op jit(solution)/shard_map/squeeze | solution.py:192
  107.1 6.7 %all-to-all-done.1.q_ref = bf16[4,4,32,1024]{3,2,1,0:T(8,128)(2,1)S(1)} async-done(((bf16[4,4,32,1024]{3,2,1,0:T(8,128)(2,1)}), bf16[4,4,32,1024]{3,2,1,0:T(8,128)(2,1)S(1)}, u32[]{:S(2)}, u32[]{:S(2)}) %all-to-all-start.1) | async-done | bytes 1048608 | tf_op jit(solution)/shard_map/all_to_all | solution.py:188
  113.8 0.0 copy-start
  113.8 1.0 copy-done
  114.8 164.9 %attend.1 = bf16[4,4,32,1024]{3,2,1,0:T(8,128)(2,1)} custom-call(s32[10]{0:T(128)} %pad_add_fusion.info, bf16[4,4,32,1024]{3,2,1,0:T(8,128)(2,1)} %copy-done, bf16[16384,128]{1,0:T(8,128)(2,1)} %get-tuple-element.6.k_hbm, bf16[16384,128]{1,0:T(8,128)(2,1)} %get-tuple-element.5.v_hbm), custom_call_target="tpu_custom_call" | custom-call | tf_op jit(solution)/shard_map/attend/pallas_call | solution.py:153
  279.6 16.2 %all_to_all.59 = bf16[4,4,32,1024]{3,2,1,0:T(8,128)(2,1)S(1)} all-to-all(bf16[4,4,32,1024]{3,2,1,0:T(8,128)(2,1)} %attend.1), channel_id=1, replica_groups=mesh['blk_0'=4,'blk_1'=4,'blk_2'=2,'uly'=4] {'blk_0'}, dimensions={0} | all-to-all | bytes 2097152 | tf_op jit(solution)/shard_map/all_to_all | solution.py:193
  295.8 0.1 copy.26
  295.9 17.3 %all_to_all.60 = bf16[4,4,32,1024]{3,2,0,1:T(8,128)(2,1)S(1)} all-to-all(bf16[4,4,32,1024]{3,2,0,1:T(8,128)(2,1)S(1)} %copy.26), channel_id=1, replica_groups=mesh['blk_0'=4,'blk_1'=4,'blk_2'=2,'uly'=4] {'uly'}, dimensions={1} | all-to-all | bytes 2097152 | tf_op jit(solution)/shard_map/all_to_all | solution.py:194
  313.2 0.8 copy.27
  314.1 1.3 copy.28
Async XLA Ops:
  6.5 94.8 %all-gather.2.cloned.1.call-start = ((), (), s32[]{:S(2)}) async-start(), calls=%async_computation.5 | async-start | bytes 8650752 | tf_op jit(solution)/shard_map/all_gather | solution.py:191
  7.5 18.1 %copy-start.1 = (s32[128]{0:T(128)S(1)}, s32[128]{0:T(128)}, u32[]{:S(2)}) copy-start(s32[128]{0:T(128)} %param.7) | copy-start | bytes 1540
  22.2 72.6 %all-to-all-start = ((bf16[4,32,4,1024]{3,1,0,2:T(8,128)(2,1)}), bf16[4,32,4,1024]{3,1,0,2:T(8,128)(2,1)S(1)}, u32[]{:S(2)}, u32[]{:S(2)}) async-start(bf16[4,32,4,1024]{3,1,0,2:T(8,128)(2,1)} %copy.22), calls=%async_computation | async-start | bytes 2097152 | tf_op jit(solution)/shard_map/all_to_all | solution.py:186
  95.8 18.0 %all-to-all-start.1 = ((bf16[4,4,32,1024]{3,2,1,0:T(8,128)(2,1)}), bf16[4,4,32,1024]{3,2,1,0:T(8,128)(2,1)S(1)}, u32[]{:S(2)}, u32[]{:S(2)}) async-start(bf16[4,4,32,1024]{3,2,1,0:T(8,128)(2,1)} %bitcast.25), calls=%async_computation.1 | async-start | bytes 2097152 | tf_op jit(solution)/shard_map/all_to_all | solution.py:188
  113.8 1.0 copy-start
Sparse Core Ops, SparseCore 0:
  19.1 52.2 all-gather.1

commit v2 on v1

v2 whole, which is shorter than its diff:
```python
import functools
import jax, jax.numpy as jnp
from jax import lax
from jax.experimental import pallas as pl
from jax.experimental.pallas import tpu as pltpu
from jax.sharding import Mesh
from jax.sharding import PartitionSpec as P

HEAD_SIZE = 128
NDOC = 8
GROUP = 8
SCALE2 = 1.4426950408889634 * HEAD_SIZE ** -0.5
ONES = 16
UNIT = 512
BIG = 2048


def doc_start(info, pos):
    low = jnp.zeros_like(pos)
    for d in range(1, NDOC):
        low = jnp.where(info[d, 0] <= pos, jnp.maximum(low, info[d, 0]), low)
    return low


def contract(a, b, da, db):
    return lax.dot_general(a, b, (((da,), (db,)), ((), ())), preferred_element_type=jnp.float32)


def attend(place, info, q_ref, kv, o_ref, kbuf, vbuf, qcat, acc, top, sems):
    D = HEAD_SIZE
    piece = q_ref.shape[1]
    tiles = pieces = RING
    rows = pieces * piece
    M = GROUP * rows
    blocks = kbuf.shape[0] // tiles
    part = blocks * UNIT
    offset, stripe = place()
    shard = UNIT // pieces

    def loads(t):
        at = pl.ds(t * blocks, blocks)
        return (
            pltpu.make_async_copy(kv.at[at, pl.ds(0, UNIT)], kbuf.at[at], sems.at[0, t]),
            pltpu.make_async_copy(kv.at[at, pl.ds(UNIT, UNIT)], vbuf.at[at], sems.at[1, t]),
        )

    for t in range(tiles):
        for c in loads(t):
            c.start()

    @pl.loop(0, tiles)
    def _(t):
        base = offset + t * part
        first = base + stripe
        last = first + (pieces - 1) * shard + piece - 1
        for c in loads(t):
            c.wait()
        low = doc_start(info, first) // UNIT
        diag = base // UNIT
        lane = lax.broadcasted_iota(jnp.int32, (1, rows), 1)
        qpos = first + (lane // piece) * shard + lane % piece
        qlow = doc_start(info, qpos)

        for g in range(GROUP):
            q = q_ref[pl.ds(t * pieces, pieces), :, g * D:(g + 1) * D].reshape(rows, D).astype(jnp.float32) * SCALE2
            high = q.astype(jnp.bfloat16)
            at = slice(g * rows, (g + 1) * rows)
            qcat[at, :D] = high
            qcat[at, D:] = (q - high.astype(jnp.float32)).astype(jnp.bfloat16)
        acc[...] = jnp.zeros_like(acc)

        def allowed(at, size):
            kpos = at + lax.broadcasted_iota(jnp.int32, (size, rows), 0)
            return (kpos <= qpos) & (kpos >= qlow)

        def masked(p, m):
            return jnp.concatenate(
                [jnp.where(m, p[:, g * rows:(g + 1) * rows], 0.0) for g in range(p.shape[1] // rows)], axis=1)

        def step(at, size):
            k = kbuf[pl.ds(at, size // UNIT)].reshape(size, D)
            v = vbuf[pl.ds(at, size // UNIT)].reshape(size, D)
            kk = jnp.concatenate([k, k], axis=1)
            vv = jnp.concatenate([v, jnp.ones((size, ONES), v.dtype)], axis=1)
            p = masked(jnp.exp2(contract(kk, qcat[...], 1, 1)), allowed(at * UNIT, size))
            acc[...] += contract(vv, p.astype(jnp.bfloat16), 0, 0)

        units = diag + 1 - low
        per = BIG // UNIT
        big = units // per

        @pl.loop(0, big)
        def _(n):
            step(low + n * per, BIG)

        size = BIG // 2
        done = low + big * per
        while size >= UNIT:
            some = (units // (size // UNIT)) % 2

            @pl.when(some == 1)
            def _(done=done, size=size):
                step(done, size)

            done = done + some * (size // UNIT)
            size //= 2

        total = acc[D:D + 8, :]
        good = jnp.min(jnp.where((total > 2.0 ** -60) & (total < 2.0 ** 118), 1.0, 0.0))

        @pl.when(good < 0.5)
        def _():
            top[...] = jnp.full_like(top, -1e30)
            acc[...] = jnp.zeros_like(acc)

            def scores(n, g):
                q = q_ref[pl.ds(t * pieces, pieces), :, pl.ds(pl.multiple_of(g * D, D), D)].reshape(rows, D)
                m = allowed(n * UNIT, UNIT)
                return jnp.where(m, contract(kbuf[n], q, 1, 1) * SCALE2, -1e30), m

            @pl.loop(low, diag + 1)
            def _(n):
                @pl.loop(0, GROUP)
                def _(g):
                    at = pl.ds(pl.multiple_of(g * rows, rows), rows)
                    s, _ = scores(n, g)
                    top[:, at] = jnp.maximum(top[:, at], jnp.max(s, axis=0, keepdims=True))

            @pl.loop(low, diag + 1)
            def _(n):
                v = vbuf[n]
                vv = jnp.concatenate([v, jnp.ones((UNIT, ONES), v.dtype)], axis=1)

                @pl.loop(0, GROUP)
                def _(g):
                    at = pl.ds(pl.multiple_of(g * rows, rows), rows)
                    s, m = scores(n, g)
                    p = jnp.where(m, jnp.exp2(s - top[:1, at]), 0.0)
                    acc[:, at] += contract(vv, p.astype(jnp.bfloat16), 0, 0)

        for g in range(GROUP):
            at = slice(g * rows, (g + 1) * rows)
            out = acc[:D, at] / acc[D:D + 1, at]
            o_ref[pl.ds(t * pieces, pieces), :, g * D:(g + 1) * D] = out.T.astype(jnp.bfloat16).reshape(pieces, piece, D)


def place():
    return (
        lax.axis_index(("blk_1", "blk_2")) * UNIT,
        lax.axis_index("blk_0") * (UNIT // RING // RING),
    )


def attention(starts, q, kv, place=place):
    M = GROUP * RING * q.shape[1]
    vm = pl.BlockSpec(memory_space=pltpu.VMEM)
    half = (kv.shape[0], UNIT, HEAD_SIZE)
    return pl.pallas_call(
        functools.partial(attend, place),
        out_shape=jax.ShapeDtypeStruct(q.shape, jnp.bfloat16),
        in_specs=[pl.BlockSpec(memory_space=pltpu.SMEM), vm, pl.BlockSpec(memory_space=pl.ANY)],
        out_specs=vm,
        scratch_shapes=[
            pltpu.VMEM(half, jnp.bfloat16),
            pltpu.VMEM(half, jnp.bfloat16),
            pltpu.VMEM((M, 2 * HEAD_SIZE), jnp.bfloat16),
            pltpu.VMEM((HEAD_SIZE + ONES, M), jnp.float32),
            pltpu.VMEM((8, M), jnp.float32),
            pltpu.SemaphoreType.DMA((2, RING)),
        ],
        compiler_params=pltpu.CompilerParams(vmem_limit_bytes=56 << 20),
        name="attend",
    )(starts, q, kv)


AXES = ("blk_0", "blk_1", "blk_2", "uly")
RING = 4
K_ROWS = UNIT
FIRST_ROWS = 768


def coordinates():
    return {axis: lax.axis_index(axis) for axis in AXES}


def shifted(at, axis, by):
    size = 2 if axis == "blk_2" else RING
    return lax.rem(at[axis] + (by + size), size)


def greet(peers):
    barrier = pltpu.get_barrier_semaphore()
    for peer in peers:
        pl.semaphore_signal(barrier, inc=1, device_id=peer, device_id_type=pl.DeviceIdType.MESH)
    pl.semaphore_wait(barrier, len(peers))


def remote(src, dst, send, recv, peer):
    return pltpu.make_async_remote_copy(
        src_ref=src, dst_ref=dst, send_sem=send, recv_sem=recv, device_id=peer,
        device_id_type=pl.DeviceIdType.MESH)


def square_peers(at):
    return [
        {"blk_0": shifted(at, "blk_0", i), "uly": shifted(at, "uly", j)}
        for i in range(RING) for j in range(RING) if i or j
    ]


def exchange(seg, q_in, k_in, v_in, q_out, kv, count_out, counts, own_sem, q_sem, z_sem, c_sem, stream_send, stream_recv, core_sem):
    D = HEAD_SIZE
    at = coordinates()
    x, y, c, z = (at[a] for a in AXES)
    rows = q_in.shape[0]
    piece = rows // RING
    width = q_in.shape[1] // RING
    greet(square_peers(at) + [{"blk_1": shifted(at, "blk_1", j)} for j in range(1, RING)] + [{"blk_2": 1 - c}])

    def block(i, j):
        return (shifted(at, "blk_0", i) * RING + shifted(at, "blk_1", j)) * 2 + c

    me = block(0, 0)
    mine = pl.ds(pl.multiple_of(z * rows, rows), rows)
    low = pl.ds(pl.multiple_of(UNIT + z * rows, rows), rows)

    def head(ref, h):
        return ref.at[:, pl.ds(pl.multiple_of(h * D, D), D)]

    own = [
        pltpu.make_async_copy(head(k_in, z), kv.at[me, mine], own_sem.at[0]),
        pltpu.make_async_copy(head(v_in, z), kv.at[me, low], own_sem.at[1]),
    ]
    for copy in own:
        copy.start()
    for j in range(1, RING):
        to = shifted(at, "uly", j)
        remote(head(k_in, to), kv.at[me, mine], z_sem.at[0], z_sem.at[1], {"uly": to}).start()
        remote(head(v_in, to), kv.at[me, low], z_sem.at[0], z_sem.at[1], {"uly": to}).start()

    def q_part(i, j):
        return q_in.at[pl.ds(pl.multiple_of(i * piece, piece), piece), pl.ds(pl.multiple_of(j * width, width), width)]

    q_own = pltpu.make_async_copy(q_part(x, z), q_out.at[x * RING + z], own_sem.at[2])
    q_own.start()

    def send_counts(phase, axis, value):
        size = 2 if axis == "blk_2" else RING
        counts[phase, 0] = value
        for j in range(1, size):
            remote(counts.at[phase, 0], counts.at[phase, size - j], c_sem.at[0, phase], c_sem.at[1, phase],
                   {axis: shifted(at, axis, j)}).start()

    def sum_counts(phase, axis):
        size = 2 if axis == "blk_2" else RING
        got = counts.at[phase, pl.ds(1, size - 1)]
        remote(got, got, c_sem.at[0, phase], c_sem.at[1, phase], {axis: shifted(at, axis, 1)}).wait()
        total = counts[phase, 0]
        for j in range(1, size):
            total = total + counts[phase, j]
        return total

    docs = lax.broadcasted_iota(jnp.int32, (NDOC, seg.shape[1]), 0)
    send_counts(0, "uly", jnp.where(seg[...] < docs, 1, 0))

    for peer in square_peers(at):
        i, j = (peer["blk_0"], peer["uly"])
        remote(q_part(i, j), q_out.at[x * RING + z], q_sem.at[0], q_sem.at[1], peer).start()

    for copy in own:
        copy.wait()
    got = kv.at[0, pl.ds(0, 2 * (RING - 1) * rows)]
    remote(got, got, z_sem.at[0], z_sem.at[1], {"uly": shifted(at, "uly", 1)}).wait()

    streams = (
        (0, 0, FIRST_ROWS, "blk_0", "blk_1"),
        (1, FIRST_ROWS, 2 * UNIT - FIRST_ROWS, "blk_1", "blk_0"),
    )
    order = (0, -1, 1, 2)

    def region(stream, i, j, half=None):
        _, start, size, first, _ = stream
        if half is not None:
            size //= 2
            start += half * size
        return kv.at[block(i, j) if first == "blk_0" else block(j, i), pl.ds(start, size)]

    def ring_copy(stream, what, axis, by, slot):
        return remote(what, what, stream_send.at[stream[0]], stream_recv.at[stream[0], slot], {axis: shifted(at, axis, by)})

    def to_core(what):
        remote(what, what, core_sem.at[0], core_sem.at[1], {"blk_2": 1 - c}).start()

    def spread(stream, axis, slot, pick):
        ring_copy(stream, pick(0), axis, 1, slot).start()
        ring_copy(stream, pick(0), axis, -1, slot + 1).start()

    def relay(stream, axis, slot, pick):
        ring_copy(stream, pick(-1), axis, 1, slot).wait_recv()
        ring_copy(stream, pick(-1, 0), axis, 1, slot + 2).start()
        ring_copy(stream, pick(1), axis, -1, slot + 1).wait_recv()
        ring_copy(stream, pick(1, 1), axis, -1, slot + 3).start()

    def settle(stream, axis, slot, pick):
        ring_copy(stream, pick(2, 0), axis, 1, slot + 2).wait_recv()
        ring_copy(stream, pick(2, 1), axis, -1, slot + 3).wait_recv()

    def along_first(stream):
        return lambda i, half=None: region(stream, i, 0, half)

    def along_second(stream, i):
        return lambda j, half=None: region(stream, i, j, half)

    for s in streams:
        spread(s, s[3], 0, along_first(s))
    for s in streams:
        spread(s, s[4], 4, along_second(s, 0))
    to_core(kv.at[me])
    send_counts(1, "blk_0", sum_counts(0, "uly"))
    for s in streams:
        relay(s, s[3], 0, along_first(s))
        for n in (1, 2):
            spread(s, s[4], 4 + 4 * n, along_second(s, order[n]))
            to_core(region(s, order[n], 0))
    send_counts(2, "blk_1", sum_counts(1, "blk_0"))
    for s in streams:
        relay(s, s[4], 4, along_second(s, 0))
        to_core(region(s, 0, -1))
        to_core(region(s, 0, 1))
    for s in streams:
        settle(s, s[3], 0, along_first(s))
        spread(s, s[4], 16, along_second(s, 2))
        to_core(region(s, 2, 0))
    send_counts(3, "blk_2", sum_counts(2, "blk_1"))
    for n in (1, 2, 3):
        for s in streams:
            settle(s, s[4], 4 * n, along_second(s, order[n - 1]))
            to_core(region(s, order[n - 1], 2))
            relay(s, s[4], 4 + 4 * n, along_second(s, order[n]))
            to_core(region(s, order[n], -1))
            to_core(region(s, order[n], 1))
    count_out[...] = jnp.broadcast_to(jnp.sum(sum_counts(3, "blk_2"), axis=1, keepdims=True), count_out.shape)
    for s in streams:
        settle(s, s[4], 16, along_second(s, 2))
        to_core(region(s, 2, 2))
    for s in streams:
        sent = kv.at[pl.ds(0, 15), pl.ds(s[1], s[2])]
        ring_copy(s, sent, s[3], 1, 0).wait_send()
    half = kv.at[pl.ds(0, 16)]
    remote(half, half, core_sem.at[0], core_sem.at[1], {"blk_2": 1 - c}).wait()
    q_own.wait()
    most = q_out.at[pl.ds(0, RING * RING - 1)]
    remote(most, most, q_sem.at[0], q_sem.at[1], {"uly": shifted(at, "uly", 1)}).wait()


def give_back(o_in, out, own_sem, sem):
    at = coordinates()
    x, z = at["blk_0"], at["uly"]
    piece, width = o_in.shape[1:]
    peers = square_peers(at)
    greet(peers)
    here = out.at[pl.ds(pl.multiple_of(x * piece, piece), piece), pl.ds(pl.multiple_of(z * width, width), width)]
    own = pltpu.make_async_copy(o_in.at[x * RING + z], here, own_sem)
    for peer in peers:
        remote(o_in.at[peer["blk_0"] * RING + peer["uly"]], here, sem.at[0], sem.at[1], peer).start()
    own.start()
    own.wait()
    most = o_in.at[pl.ds(0, RING * RING - 1)]
    remote(most, most, sem.at[0], sem.at[1], peers[0]).wait()


def local(queries, keys, values, segments):
    rows, wide = queries.shape
    piece, width = rows // RING, wide // RING
    anywhere = pl.BlockSpec(memory_space=pl.ANY)
    vm = pl.BlockSpec(memory_space=pltpu.VMEM)
    q, kv, starts = pl.pallas_call(
        exchange,
        out_shape=(
            jax.ShapeDtypeStruct((RING * RING, piece, width), jnp.bfloat16),
            jax.ShapeDtypeStruct((2 * RING * RING, 2 * UNIT, HEAD_SIZE), jnp.bfloat16),
            jax.ShapeDtypeStruct((NDOC, 128), jnp.int32),
        ),
        in_specs=[vm, anywhere, anywhere, anywhere],
        out_specs=(anywhere, anywhere, vm),
        scratch_shapes=[
            pltpu.VMEM((4, RING, NDOC, rows), jnp.int32),
            pltpu.SemaphoreType.DMA((3,)),
            pltpu.SemaphoreType.DMA((2,)),
            pltpu.SemaphoreType.DMA((2,)),
            pltpu.SemaphoreType.DMA((2, 4)),
            pltpu.SemaphoreType.DMA((2,)),
            pltpu.SemaphoreType.DMA((2, 20)),
            pltpu.SemaphoreType.DMA((2,)),
        ],
        compiler_params=pltpu.CompilerParams(collective_id=0, has_side_effects=True),
        name="exchange",
    )(segments.reshape(1, rows), queries, keys, values)
    out = attention(starts, q, kv)
    return pl.pallas_call(
        give_back,
        out_shape=jax.ShapeDtypeStruct((rows, wide), jnp.bfloat16),
        in_specs=[anywhere],
        out_specs=anywhere,
        scratch_shapes=[pltpu.SemaphoreType.DMA, pltpu.SemaphoreType.DMA((2,))],
        compiler_params=pltpu.CompilerParams(collective_id=1, has_side_effects=True),
        name="give_back",
    )(out)


def solution(mesh):
    split = Mesh(mesh.devices.reshape(4, 4, 2, mesh.shape["uly"]), AXES)
    return jax.shard_map(
        local,
        mesh=split,
        in_specs=(P(AXES, None), P(AXES, None), P(AXES, None), P(AXES)),
        out_specs=P(AXES, None),
        check_vma=False,
    )
```

time: 326 us -> 261 us (0.80)
  blocking collectives: 112 us -> 0 us
  Pallas kernels: 165 us -> 257 us
  between operations: 13.5 us -> 0.02 us
  local copies, waits for them, and re-layouts: 14.1 us -> 2.29 us
  starting transfers between devices: 9.09 us -> 0 us
  waiting for transfers between devices: 6.74 us -> 0 us
    pallas_call x1 -> x3, Pallas kernels: 165 us -> 257 us  [the longest x1 188 us: attention(): pl.pallas_call(functools.partial(attend, place), out_shape=jax.ShapeDtype...]
    psum x1 -> x0, blocking collectives: 68.3 us -> none  [local(): starts = lax.psum(counts, BLK_ULY)]
    all_to_all x3 -> x0, blocking collectives: 43.9 us -> none  [the longest x1 17.3 us: local(): out = lax.all_to_all(out, 'uly', split_axis=1, concat_axis=3, tiled=True)]
    all_to_all x2 -> x0, starting transfers between devices: 9.09 us -> none  [the longest x1 5.57 us: local(): q = lax.all_to_all(q, 'blk_0', split_axis=0, concat_axis=0, tiled=True)]
    all_to_all x2 -> x0, waiting for transfers between devices: 6.72 us -> none  [the longest x1 6.72 us: local(): q = lax.all_to_all(q, 'blk_0', split_axis=0, concat_axis=0, tiled=True)]
    squeeze x1 -> x0, local copies, waits for them, and re-layouts: 5.68 us -> none  [local(): out = attention(info, q, kv[0], kv[1])]
  transfers between devices with their start and end apart: 3 -> 0, of which waited for: 1 -> 0; matrix products, arithmetic and copies ran while one was open for 3% -> 0% of each run, Pallas kernels for 0% -> 0%
where the time goes in v2:
time: 261 us; the launch traced here: 259 us
  Pallas kernels  257 us (98%)
    pallas_call x1, Pallas kernels, attention(): pl.pallas_call(functools.partial(attend, place), out_shape=jax.ShapeDtype...  188 us
    pallas_call x1, Pallas kernels, local(): pl.pallas_call(exchange, out_shape=(jax.ShapeDtypeStruct((RING * RING, pi...  57.4 us
    pallas_call x1, Pallas kernels, local(): pl.pallas_call(give_back, out_shape=jax.ShapeDtypeStruct((rows, wide), jn...  11.9 us

profile of v2, /device:TPU:31, one launch (start us, length us, event | category | flops | bytes accessed | tf_op | source)
XLA Modules:
  0.0 259.3 jit_solution(18428159926986555270)
XLA Ops:
  0.0 57.4 %exchange.1 = (bf16[16,32,1024]{2,1,0:T(8,128)(2,1)}, bf16[32,1024,128]{2,1,0:T(8,128)(2,1)}, s32[8,128]{1,0:T(8,128)}) custom-call(s32[1,128]{1,0:T(1,128)} %bitcast.1, bf16[128,4096]{1,0:T(8,128)(2,1)} %q_in.1, bf16[128,512]{1,0:T(8,128)(2,1)} %k_in.1, bf16[128,512]{1,0:T(8,128)(2,1)} %v_in.1), custom_call_target="tpu_custom_call" | custom-call | tf_op jit(solution)/shard_map/exchange/pallas_call | solution.py:377
  57.5 187.7 %attend.1.o_in = bf16[16,32,1024]{2,1,0:T(8,128)(2,1)} custom-call(s32[8,128]{1,0:T(8,128)} %get-tuple-element.8.info, bf16[16,32,1024]{2,1,0:T(8,128)(2,1)} %get-tuple-element.9.q_ref, bf16[32,1024,128]{2,1,0:T(8,128)(2,1)} %get-tuple-element.10.kv), custom_call_target="tpu_custom_call" | custom-call | tf_op jit(solution)/shard_map/attend/pallas_call | solution.py:158
  245.1 11.9 %give_back.1 = bf16[128,4096]{1,0:T(8,128)(2,1)} custom-call(bf16[16,32,1024]{2,1,0:T(8,128)(2,1)} %attend.1.o_in), custom_call_target="tpu_custom_call" | custom-call | tf_op jit(solution)/shard_map/give_back/pallas_call | solution.py:400
  257.0 2.3 copy.6

commit v3 on v2

--- a/solution.py
+++ b/solution.py
@@ -369,7 +369,7 @@
     remote(most, most, sem.at[0], sem.at[1], peers[0]).wait()
 
 
-def local(queries, keys, values, segments):
+def careful(queries, keys, values, segments):
     rows, wide = queries.shape
     piece, width = rows // RING, wide // RING
     anywhere = pl.BlockSpec(memory_space=pl.ANY)
@@ -393,7 +393,7 @@
             pltpu.SemaphoreType.DMA((2, 20)),
             pltpu.SemaphoreType.DMA((2,)),
         ],
-        compiler_params=pltpu.CompilerParams(collective_id=0, has_side_effects=True),
+        compiler_params=pltpu.CompilerParams(collective_id=1, has_side_effects=True),
         name="exchange",
     )(segments.reshape(1, rows), queries, keys, values)
     out = attention(starts, q, kv)
@@ -403,9 +403,285 @@
         in_specs=[anywhere],
         out_specs=anywhere,
         scratch_shapes=[pltpu.SemaphoreType.DMA, pltpu.SemaphoreType.DMA((2,))],
-        compiler_params=pltpu.CompilerParams(collective_id=1, has_side_effects=True),
+        compiler_params=pltpu.CompilerParams(collective_id=2, has_side_effects=True),
         name="give_back",
     )(out)
+
+
+COLUMN = 2 * UNIT
+REACH = 8
+CHUNK = 2080
+CHUNKS = 4
+WAITS = (
+    (0, (1, 2), (0, 1, 2)),
+    (1, (8,), ()),
+    (2, (3,), ()),
+    (4, (), (3, 4)),
+    (6, (5, 6), ()),
+    (7, (7,), ()),
+    (8, (), (5, 6)),
+    (9, (), (7, 8)),
+)
+LIMIT = 100.0
+
+
+def ring_attend(seg, q_in, k_in, v_in, out, stats_out, kv, qbuf, obuf, qv, kv_own, qcat, acc, stats,
+                local_sem, bar_z, q_sem, s_sem, send_sem, recv_sem, core_send, core_recv, o_sem):
+    D = HEAD_SIZE
+    x, y, c, z = (lax.axis_index(a) for a in AXES)
+    column = x * RING + y
+    rows = q_in.shape[0]
+    width = q_in.shape[1] // RING
+
+    def peer(axis, by):
+        size = 2 if axis == "blk_2" else RING
+        return {axis: lax.rem(lax.axis_index(axis) + by, size)}
+
+    barrier = pltpu.get_barrier_semaphore()
+    for axis in AXES:
+        for by in range(1, 2 if axis == "blk_2" else RING):
+            pl.semaphore_signal(barrier, inc=1, device_id=peer(axis, by), device_id_type=pl.DeviceIdType.MESH)
+    pl.semaphore_wait(barrier, 10)
+
+    def place(d, core):
+        return pl.ds(pl.multiple_of((REACH - d) * COLUMN + core * UNIT, UNIT), UNIT)
+
+    mine = pl.ds(pl.multiple_of(REACH * COLUMN + c * UNIT + z * rows, rows), rows)
+
+    def head(ref, h, size):
+        return ref.at[:, pl.ds(pl.multiple_of(h * size, size), size)]
+
+    for j in (1, 3, 2):
+        to = peer("uly", j)
+        remote(head(k_in, to["uly"], D), kv.at[0, mine], bar_z.at[0], bar_z.at[1], to).start()
+        remote(head(v_in, to["uly"], D), kv.at[1, mine], bar_z.at[0], bar_z.at[1], to).start()
+    own = [
+        pltpu.make_async_copy(head(k_in, z, D), kv.at[0, mine], local_sem.at[0]),
+        pltpu.make_async_copy(head(v_in, z, D), kv.at[1, mine], local_sem.at[1]),
+        pltpu.make_async_copy(head(q_in, z, width), qbuf.at[0], local_sem.at[2]),
+        pltpu.make_async_copy(q_in, qv, local_sem.at[3]),
+        pltpu.make_async_copy(k_in, kv_own, local_sem.at[4]),
+    ]
+    for copy in own:
+        copy.start()
+    for j in (1, 3, 2):
+        to = peer("uly", j)
+        remote(head(q_in, to["uly"], width), qbuf.at[RING - j], q_sem.at[0, j], q_sem.at[1, RING - j], to).start()
+
+    @pl.loop(1, REACH + 1)
+    def _(d):
+        @pl.when(column < d)
+        def _():
+            at = pl.ds(pl.multiple_of((REACH - d) * COLUMN, COLUMN), COLUMN)
+            kv[0, at] = jnp.zeros((COLUMN, D), kv.dtype)
+            kv[1, at] = jnp.zeros((COLUMN, D), kv.dtype)
+
+    own[3].wait()
+    own[4].wait()
+
+    def longest(ref):
+        most = jnp.zeros((rows, 1), jnp.float32)
+        for h in range(ref.shape[1] // D):
+            a = ref[:, h * D:(h + 1) * D].astype(jnp.float32)
+            most = jnp.maximum(most, jnp.sum(a * a, axis=1, keepdims=True))
+        return jnp.broadcast_to(jnp.max(most, axis=0, keepdims=True), (1, rows))
+
+    kind = lax.broadcasted_iota(jnp.int32, (2 * NDOC, rows), 0)
+    before = jnp.where(seg[...] < kind, 1.0, 0.0)
+    before = jnp.where(kind == NDOC, longest(qv), jnp.where(kind > NDOC, longest(kv_own), before))
+
+    def send_stats(phase, axis, value):
+        size = 2 if axis == "blk_2" else RING
+        stats[phase, 0] = value
+        for j in range(1, size):
+            remote(stats.at[phase, 0], stats.at[phase, size - j], s_sem.at[0, phase], s_sem.at[1, phase], peer(axis, j)).start()
+
+    def sum_stats(phase, axis):
+        size = 2 if axis == "blk_2" else RING
+        got = stats.at[phase, pl.ds(1, size - 1)]
+        remote(got, got, s_sem.at[0, phase], s_sem.at[1, phase], peer(axis, 1)).wait()
+        total = stats[phase, 0]
+        for j in range(1, size):
+            other = stats[phase, j]
+            total = jnp.where(kind < NDOC, total + other, jnp.maximum(total, other))
+        return total
+
+    send_stats(0, "uly", before)
+    own[0].wait()
+    own[1].wait()
+    got = kv.at[0, pl.ds(0, 2 * (RING - 1) * rows)]
+    remote(got, got, bar_z.at[0], bar_z.at[1], peer("uly", 1)).wait()
+
+    def move(n, from_d, to_d, to):
+        return remote(kv.at[:, place(from_d, c)], kv.at[:, place(to_d, c)], send_sem.at[n], recv_sem.at[to_d], to)
+
+    moves = []
+
+    def start_if(able, *what):
+        moves.append((able, what))
+
+        @pl.when(able)
+        def _():
+            move(*what).start()
+
+    def received(d):
+        @pl.when(column >= d)
+        def _():
+            move(0, d, d, {"blk_1": y}).wait_recv()
+            to_core(d).start()
+
+    def to_core(d):
+        what = kv.at[:, place(d, c)]
+        return remote(what, what, core_send.at[d], core_recv.at[d], {"blk_2": 1 - c})
+
+    def from_core(d):
+        @pl.when(column >= d)
+        def _():
+            to_core(d).wait_recv()
+
+    start_if(x < 3, 0, 0, 4, peer("blk_0", 1))
+    start_if(x < 2, 1, 0, 8, peer("blk_0", 2))
+    for j in (1, 3, 2):
+        start_if(y + j < RING, 1 + j, 0, j, peer("blk_1", j))
+    to_core(0).start()
+    send_stats(1, "blk_0", sum_stats(0, "uly"))
+    received(4)
+    for j in (1, 3, 2):
+        to = peer("blk_1", j)
+        start_if(x >= 1, 4 + j, 4, 4 + to["blk_1"] - y, to)
+    send_stats(2, "blk_1", sum_stats(1, "blk_0"))
+
+    far = [((x >= 2) & (y >= j), (7 + j, 8, 8 - j, peer("blk_1", RING - j))) for j in (1, 3, 2)]
+    moves.extend(far)
+
+    def relay_far():
+        for able, what in far:
+            @pl.when(able)
+            def _(what=what):
+                move(*what).start()
+
+    send_stats(3, "blk_2", sum_stats(2, "blk_1"))
+    final = sum_stats(3, "blk_2")
+    reach = final[NDOC:NDOC + 1] * final[NDOC + 1:NDOC + 2] * SCALE2 ** 2
+    stats_out[...] = jnp.broadcast_to(jnp.where(reach < LIMIT ** 2, 1, 0), stats_out.shape)
+    starts = jnp.sum(final[:NDOC], axis=1, keepdims=True).astype(jnp.int32)
+    starts = jnp.broadcast_to(starts, (NDOC, rows))
+    own[2].wait()
+
+    @pl.loop(0, RING * CHUNKS)
+    def _(n):
+        early = n < 2 * RING
+        turn = jnp.where(early, n % RING, (n - 2 * RING) // 2)
+        chunk = jnp.where(early, n // RING, 2 + n % 2)
+        to = lax.rem(z + turn, RING)
+
+        for at_step, arrivals, crossed in WAITS:
+            @pl.when(n == at_step)
+            def _(arrivals=arrivals, crossed=crossed):
+                for d in arrivals:
+                    received(d)
+                    if d == REACH:
+                        relay_far()
+                for d in crossed:
+                    from_core(d)
+
+        @pl.when(chunk == 0)
+        def _():
+            @pl.when(turn > 0)
+            def _():
+                remote(qbuf.at[turn], qbuf.at[turn], q_sem.at[0, turn], q_sem.at[1, turn], {"uly": to}).wait_recv()
+
+            for g in range(GROUP):
+                q = qbuf[turn, :, g * D:(g + 1) * D].astype(jnp.float32) * SCALE2
+                high = q.astype(jnp.bfloat16)
+                at = slice(g * rows, (g + 1) * rows)
+                qcat[turn, at, :D] = high
+                qcat[turn, at, D:] = (q - high.astype(jnp.float32)).astype(jnp.bfloat16)
+            acc[turn] = jnp.zeros(acc.shape[1:], acc.dtype)
+
+        qpos = column * COLUMN + c * UNIT + to * rows + lax.broadcasted_iota(jnp.int32, (1, rows), 1)
+        qlow = jnp.zeros_like(qpos)
+        for d in range(1, NDOC):
+            qlow = jnp.where(starts[d:d + 1] <= qpos, jnp.maximum(qlow, starts[d:d + 1]), qlow)
+        first = c * UNIT + to * rows + (CHUNKS - 1 - chunk) * CHUNK
+        at = pl.ds(pl.multiple_of(first, 32), CHUNK)
+        kpos = (column - REACH) * COLUMN + first + lax.broadcasted_iota(jnp.int32, (CHUNK, rows), 0)
+        allowed = (kpos <= qpos) & (kpos >= qlow)
+        k = kv[0, at]
+        v = kv[1, at]
+        kk = jnp.concatenate([k, k], axis=1)
+        vv = jnp.concatenate([v, jnp.ones((CHUNK, ONES), v.dtype)], axis=1)
+        p = jnp.exp2(contract(kk, qcat[turn], 1, 1))
+        p = jnp.concatenate([jnp.where(allowed, p[:, g * rows:(g + 1) * rows], 0.0) for g in range(GROUP)], axis=1)
+        acc[turn] += contract(vv, p.astype(jnp.bfloat16), 0, 0)
+
+        @pl.when(chunk == CHUNKS - 1)
+        def _():
+            for g in range(GROUP):
+                a = slice(g * rows, (g + 1) * rows)
+                o = acc[turn, :D, a] / acc[turn, D:D + 1, a]
+                obuf[turn, :, g * D:(g + 1) * D] = o.T.astype(jnp.bfloat16)
+
+            @pl.when(turn == 0)
+            def _():
+                pltpu.make_async_copy(obuf.at[0], head(out, z, width), local_sem.at[5]).start()
+
+            @pl.when(turn > 0)
+            def _():
+                remote(obuf.at[turn], head(out, z, width), o_sem.at[0], o_sem.at[1], {"uly": to}).start()
+
+    for able, what in moves:
+        @pl.when(able)
+        def _(what=what):
+            move(*what).wait_send()
+    for d in range(REACH + 1):
+        @pl.when(column >= d)
+        def _(d=d):
+            to_core(d).wait_send()
+    for j in range(1, RING):
+        remote(qbuf.at[j], qbuf.at[j], q_sem.at[0, j], q_sem.at[1, j], peer("uly", j)).wait_send()
+    pltpu.make_async_copy(obuf.at[0], head(out, z, width), local_sem.at[5]).wait()
+    got = obuf.at[pl.ds(1, RING - 1)]
+    remote(got, got, o_sem.at[0], o_sem.at[1], peer("uly", 1)).wait()
+
+
+def local(queries, keys, values, segments):
+    rows, wide = queries.shape
+    width = wide // RING
+    M = GROUP * rows
+    anywhere = pl.BlockSpec(memory_space=pl.ANY)
+    vm = pl.BlockSpec(memory_space=pltpu.VMEM)
+    out, stats = pl.pallas_call(
+        ring_attend,
+        out_shape=(
+            jax.ShapeDtypeStruct((rows, wide), jnp.bfloat16),
+            jax.ShapeDtypeStruct((8, rows), jnp.int32),
+        ),
+        in_specs=[vm, anywhere, anywhere, anywhere],
+        out_specs=(anywhere, vm),
+        scratch_shapes=[
+            pltpu.VMEM((2, (REACH + 1) * COLUMN, HEAD_SIZE), jnp.bfloat16),
+            pltpu.VMEM((RING, rows, width), jnp.bfloat16),
+            pltpu.VMEM((RING, rows, width), jnp.bfloat16),
+            pltpu.VMEM((rows, wide), jnp.bfloat16),
+            pltpu.VMEM((rows, RING * HEAD_SIZE), jnp.bfloat16),
+            pltpu.VMEM((RING, M, 2 * HEAD_SIZE), jnp.bfloat16),
+            pltpu.VMEM((RING, HEAD_SIZE + ONES, M), jnp.float32),
+            pltpu.VMEM((4, RING, 2 * NDOC, rows), jnp.float32),
+            pltpu.SemaphoreType.DMA((6,)),
+            pltpu.SemaphoreType.DMA((2,)),
+            pltpu.SemaphoreType.DMA((2, RING)),
+            pltpu.SemaphoreType.DMA((2, 4)),
+            pltpu.SemaphoreType.DMA((11,)),
+            pltpu.SemaphoreType.DMA((REACH + 1,)),
+            pltpu.SemaphoreType.DMA((REACH + 1,)),
+            pltpu.SemaphoreType.DMA((REACH + 1,)),
+            pltpu.SemaphoreType.DMA((2,)),
+        ],
+        compiler_params=pltpu.CompilerParams(collective_id=0, has_side_effects=True, vmem_limit_bytes=56 << 20),
+        name="ring_attend",
+    )(segments.reshape(1, rows), queries, keys, values)
+    return lax.cond(stats[0, 0] == 1, lambda *_: out, careful, queries, keys, values, segments)
 
 
 def solution(mesh):

time: 261 us -> 367 us (1.41)
  the two profiles are of different devices: /device:TPU:31 before, /device:TPU:24 now
where the time goes in v3:
time: 367 us
  Pallas kernels  364 us (99%)
    pallas_call x1, Pallas kernels, attention(): pl.pallas_call(functools.partial(attend, place), out_shape=jax.ShapeDtype...  211 us
    pallas_call x1, Pallas kernels, local(): pl.pallas_call(ring_attend, out_shape=(jax.ShapeDtypeStruct((rows, wide),...  77.2 us
    pallas_call x1, Pallas kernels, careful(): pl.pallas_call(exchange, out_shape=(jax.ShapeDtypeStruct((RING * RING, pi...  63 us
    pallas_call x1, Pallas kernels, careful(): pl.pallas_call(give_back, out_shape=jax.ShapeDtypeStruct((rows, wide), jn...  12.8 us

profile of v3, /device:TPU:24, one launch (start us, length us, event | category | flops | bytes accessed | tf_op | source)
XLA Modules:
  0.0 366.5 jit_solution(13135237645915567119)
XLA Ops:
  0.0 77.2 %ring_attend.1 = (bf16[128,4096]{1,0:T(8,128)(2,1)S(1)}, s32[8,128]{1,0:T(8,128)}) custom-call(s32[1,128]{1,0:T(1,128)} %bitcast.3, bf16[128,4096]{1,0:T(8,128)(2,1)} %q_in.1, bf16[128,512]{1,0:T(8,128)(2,1)} %k_in.1, bf16[128,512]{1,0:T(8,128)(2,1)} %v_in.1), custom_call_target="tpu_custom_call" | custom-call | tf_op jit(solution)/shard_map/ring_attend/pallas_call | solution.py:654
  77.2 1.2 slice.3
  79.1 286.5 %conditional.1 = (bf16[128,4096]{1,0:T(8,128)(2,1)S(1)}) conditional(s32[]{:T(128)} %bitcast.2, (s32[128]{0:T(128)}, bf16[128,4096]{1,0:T(8,128)(2,1)}, bf16[128,512]{1,0:T(8,128)(2,1)}, bf16[128,512]{1,0:T(8,128)(2,1)}) %tuple.11, bf16[128,4096]{1,0:T(8,128)(2,1)S(1)} %get-tuple-element.27), branch_computations={%region_0.0_spmd, %region_1.0_spmd} | conditional | bytes 8 | solution.py:684
  79.1 63.0 %exchange.1 = (bf16[16,32,1024]{2,1,0:T(8,128)(2,1)}, bf16[32,1024,128]{2,1,0:T(8,128)(2,1)}, s32[8,128]{1,0:T(8,128)}) custom-call(s32[1,128]{1,0:T(1,128)} %bitcast.4, bf16[128,4096]{1,0:T(8,128)(2,1)} %get-tuple-element.18.q_in, bf16[128,512]{1,0:T(8,128)(2,1)} %get-tuple-element.19.k_in, bf16[128,512]{1,0:T(8,128)(2,1)} %get-tuple-element.20.v_in), custom_call_target="tpu_custom_call" | custom-call | tf_op jit(solution)/shard_map/cond/branch_0_fun/exchange/pallas_call | solution.py:377
  142.1 210.6 %attend.1.o_in = bf16[16,32,1024]{2,1,0:T(8,128)(2,1)} custom-call(s32[8,128]{1,0:T(8,128)} %get-tuple-element.21.info, bf16[16,32,1024]{2,1,0:T(8,128)(2,1)} %get-tuple-element.22.q_ref, bf16[32,1024,128]{2,1,0:T(8,128)(2,1)} %get-tuple-element.23.kv), custom_call_target="tpu_custom_call" | custom-call | tf_op jit(solution)/shard_map/cond/branch_0_fun/attend/pallas_call | solution.py:158
  352.7 12.8 %give_back.1 = bf16[128,4096]{1,0:T(8,128)(2,1)S(1)} custom-call(bf16[16,32,1024]{2,1,0:T(8,128)(2,1)} %attend.1.o_in), custom_call_target="tpu_custom_call" | custom-call | tf_op jit(solution)/shard_map/cond/branch_0_fun/give_back/pallas_call | solution.py:400
  365.5 1.0 copy.10

commit v4 on v3

--- a/solution.py
+++ b/solution.py
@@ -413,14 +413,14 @@
 CHUNK = 2080
 CHUNKS = 4
 WAITS = (
-    (0, (1, 2), (0, 1, 2)),
-    (1, (8,), ()),
-    (2, (3,), ()),
-    (4, (), (3, 4)),
-    (6, (5, 6), ()),
-    (7, (7,), ()),
-    (8, (), (5, 6)),
-    (9, (), (7, 8)),
+    (0, (1, 2), (0, 1, 2), 3),
+    (2, (3,), (), 0),
+    (3, (8,), (), 3),
+    (4, (), (3, 4), 0),
+    (6, (5, 6), (), 0),
+    (7, (7,), (), 0),
+    (8, (), (5, 6), 0),
+    (9, (), (7, 8), 0),
 )
 LIMIT = 100.0
 
@@ -437,11 +437,14 @@
         size = 2 if axis == "blk_2" else RING
         return {axis: lax.rem(lax.axis_index(axis) + by, size)}
 
-    barrier = pltpu.get_barrier_semaphore()
-    for axis in AXES:
-        for by in range(1, 2 if axis == "blk_2" else RING):
-            pl.semaphore_signal(barrier, inc=1, device_id=peer(axis, by), device_id_type=pl.DeviceIdType.MESH)
-    pl.semaphore_wait(barrier, 10)
+    def group(phase):
+        if phase == 0:
+            return [peer("uly", j) for j in range(1, RING)]
+        if phase == 2:
+            return [peer("blk_0", j) for j in range(1, RING)]
+        return [{**peer("blk_1", j % RING), **peer("blk_2", j // RING)} for j in range(1, 2 * RING)]
+
+    greet(group(0) + group(1) + group(2))
 
     def place(d, core):
         return pl.ds(pl.multiple_of((REACH - d) * COLUMN + core * UNIT, UNIT), UNIT)
@@ -464,10 +467,6 @@
     ]
     for copy in own:
         copy.start()
-    for j in (1, 3, 2):
-        to = peer("uly", j)
-        remote(head(q_in, to["uly"], width), qbuf.at[RING - j], q_sem.at[0, j], q_sem.at[1, RING - j], to).start()
-
     @pl.loop(1, REACH + 1)
     def _(d):
         @pl.when(column < d)
@@ -490,27 +489,33 @@
     before = jnp.where(seg[...] < kind, 1.0, 0.0)
     before = jnp.where(kind == NDOC, longest(qv), jnp.where(kind > NDOC, longest(kv_own), before))
 
-    def send_stats(phase, axis, value):
-        size = 2 if axis == "blk_2" else RING
+    def send_stats(phase, value):
         stats[phase, 0] = value
-        for j in range(1, size):
-            remote(stats.at[phase, 0], stats.at[phase, size - j], s_sem.at[0, phase], s_sem.at[1, phase], peer(axis, j)).start()
-
-    def sum_stats(phase, axis):
-        size = 2 if axis == "blk_2" else RING
+        to = group(phase)
+        for n, target in enumerate(to):
+            slot = (n + 1) % RING + (n + 1) // RING * RING
+            slot = (RING - slot % RING) % RING + slot // RING * RING
+            remote(stats.at[phase, 0], stats.at[phase, slot], s_sem.at[0, phase], s_sem.at[1, phase], target).start()
+
+    def sum_stats(phase):
+        size = len(group(phase)) + 1
         got = stats.at[phase, pl.ds(1, size - 1)]
-        remote(got, got, s_sem.at[0, phase], s_sem.at[1, phase], peer(axis, 1)).wait()
+        remote(got, got, s_sem.at[0, phase], s_sem.at[1, phase], group(phase)[0]).wait()
         total = stats[phase, 0]
         for j in range(1, size):
             other = stats[phase, j]
             total = jnp.where(kind < NDOC, total + other, jnp.maximum(total, other))
         return total
 
-    send_stats(0, "uly", before)
+    send_stats(0, before)
     own[0].wait()
     own[1].wait()
     got = kv.at[0, pl.ds(0, 2 * (RING - 1) * rows)]
     remote(got, got, bar_z.at[0], bar_z.at[1], peer("uly", 1)).wait()
+    for j in (1, 3, 2):
+        to = peer("uly", j)
+        remote(head(q_in, to["uly"], width), qbuf.at[RING - j], q_sem.at[0, j], q_sem.at[1, RING - j], to).start()
+
 
     def move(n, from_d, to_d, to):
         return remote(kv.at[:, place(from_d, c)], kv.at[:, place(to_d, c)], send_sem.at[n], recv_sem.at[to_d], to)
@@ -539,29 +544,35 @@
         def _():
             to_core(d).wait_recv()
 
-    start_if(x < 3, 0, 0, 4, peer("blk_0", 1))
-    start_if(x < 2, 1, 0, 8, peer("blk_0", 2))
-    for j in (1, 3, 2):
-        start_if(y + j < RING, 1 + j, 0, j, peer("blk_1", j))
-    to_core(0).start()
-    send_stats(1, "blk_0", sum_stats(0, "uly"))
-    received(4)
-    for j in (1, 3, 2):
-        to = peer("blk_1", j)
-        start_if(x >= 1, 4 + j, 4, 4 + to["blk_1"] - y, to)
-    send_stats(2, "blk_1", sum_stats(1, "blk_0"))
-
-    far = [((x >= 2) & (y >= j), (7 + j, 8, 8 - j, peer("blk_1", RING - j))) for j in (1, 3, 2)]
-    moves.extend(far)
-
-    def relay_far():
-        for able, what in far:
+    later = []
+
+    def start_later(able, *what):
+        moves.append((able, what))
+        later.append((able, what))
+
+    def flush(count):
+        for _ in range(count):
+            able, what = later.pop(0)
+
             @pl.when(able)
             def _(what=what):
                 move(*what).start()
 
-    send_stats(3, "blk_2", sum_stats(2, "blk_1"))
-    final = sum_stats(3, "blk_2")
+    send_stats(1, sum_stats(0))
+    for j in (1, 2, 3):
+        start_if(y + j < RING, 1 + j, 0, j, peer("blk_1", j))
+    start_if(x < 3, 0, 0, 4, peer("blk_0", 1))
+    to_core(0).start()
+    send_stats(2, sum_stats(1))
+    received(4)
+    start_if((x >= 1) & (x < 3), 1, 4, 8, peer("blk_0", 1))
+    for j in (1, 2, 3):
+        start_if((x >= 1) & (y >= j), 4 + j, 4, 4 - j, peer("blk_1", RING - j))
+    for j in (1, 2, 3):
+        start_later((x >= 1) & (y + j < RING), 10 + j, 4, 4 + j, peer("blk_1", j))
+    for j in (1, 2, 3):
+        start_later((x >= 2) & (y >= j), 7 + j, 8, 8 - j, peer("blk_1", RING - j))
+    final = sum_stats(2)
     reach = final[NDOC:NDOC + 1] * final[NDOC + 1:NDOC + 2] * SCALE2 ** 2
     stats_out[...] = jnp.broadcast_to(jnp.where(reach < LIMIT ** 2, 1, 0), stats_out.shape)
     starts = jnp.sum(final[:NDOC], axis=1, keepdims=True).astype(jnp.int32)
@@ -571,19 +582,19 @@
     @pl.loop(0, RING * CHUNKS)
     def _(n):
         early = n < 2 * RING
-        turn = jnp.where(early, n % RING, (n - 2 * RING) // 2)
+        last = (n - 2 * RING) // 2
+        turn = jnp.where(early, n % RING, jnp.where(last == 0, 2, jnp.where(last == RING - 1, 0, 2 * last - 1)))
         chunk = jnp.where(early, n // RING, 2 + n % 2)
         to = lax.rem(z + turn, RING)
 
-        for at_step, arrivals, crossed in WAITS:
+        for at_step, arrivals, crossed, count in WAITS:
             @pl.when(n == at_step)
-            def _(arrivals=arrivals, crossed=crossed):
+            def _(arrivals=arrivals, crossed=crossed, count=count):
                 for d in arrivals:
                     received(d)
-                    if d == REACH:
-                        relay_far()
                 for d in crossed:
                     from_core(d)
+                flush(count)
 
         @pl.when(chunk == 0)
         def _():
@@ -667,12 +678,12 @@
             pltpu.VMEM((rows, RING * HEAD_SIZE), jnp.bfloat16),
             pltpu.VMEM((RING, M, 2 * HEAD_SIZE), jnp.bfloat16),
             pltpu.VMEM((RING, HEAD_SIZE + ONES, M), jnp.float32),
-            pltpu.VMEM((4, RING, 2 * NDOC, rows), jnp.float32),
+            pltpu.VMEM((3, 2 * RING, 2 * NDOC, rows), jnp.float32),
             pltpu.SemaphoreType.DMA((6,)),
             pltpu.SemaphoreType.DMA((2,)),
             pltpu.SemaphoreType.DMA((2, RING)),
             pltpu.SemaphoreType.DMA((2, 4)),
-            pltpu.SemaphoreType.DMA((11,)),
+            pltpu.SemaphoreType.DMA((14,)),
             pltpu.SemaphoreType.DMA((REACH + 1,)),
             pltpu.SemaphoreType.DMA((REACH + 1,)),
             pltpu.SemaphoreType.DMA((REACH + 1,)),

time: 367 us -> 373 us (1.016)
  Pallas kernels: 364 us -> 370 us
    pallas_call x1, Pallas kernels: 211 us -> 227 us  [attention(): pl.pallas_call(functools.partial(attend, place), out_shape=jax.ShapeDtype...]
    pallas_call x1, Pallas kernels: 77.2 us -> 63 us  [local(): pl.pallas_call(ring_attend, out_shape=(jax.ShapeDtypeStruct((rows, wide),...]
    pallas_call x1, Pallas kernels: 63 us -> 67 us  [careful(): pl.pallas_call(exchange, out_shape=(jax.ShapeDtypeStruct((RING * RING, pi...]
where the time goes in v4:
time: 373 us
  Pallas kernels  370 us (99%)
    pallas_call x1, Pallas kernels, attention(): pl.pallas_call(functools.partial(attend, place), out_shape=jax.ShapeDtype...  227 us
    pallas_call x1, Pallas kernels, careful(): pl.pallas_call(exchange, out_shape=(jax.ShapeDtypeStruct((RING * RING, pi...  67 us
    pallas_call x1, Pallas kernels, local(): pl.pallas_call(ring_attend, out_shape=(jax.ShapeDtypeStruct((rows, wide),...  63 us
    pallas_call x1, Pallas kernels, careful(): pl.pallas_call(give_back, out_shape=jax.ShapeDtypeStruct((rows, wide), jn...  12.8 us

profile of v4, /device:TPU:24, one launch (start us, length us, event | category | flops | bytes accessed | tf_op | source)
XLA Modules:
  0.0 373.1 jit_solution(3122972682725611207)
XLA Ops:
  0.0 63.0 %ring_attend.1 = (bf16[128,4096]{1,0:T(8,128)(2,1)S(1)}, s32[8,128]{1,0:T(8,128)}) custom-call(s32[1,128]{1,0:T(1,128)} %bitcast.3, bf16[128,4096]{1,0:T(8,128)(2,1)} %q_in.1, bf16[128,512]{1,0:T(8,128)(2,1)} %k_in.1, bf16[128,512]{1,0:T(8,128)(2,1)} %v_in.1), custom_call_target="tpu_custom_call" | custom-call | tf_op jit(solution)/shard_map/ring_attend/pallas_call | solution.py:665
  63.0 1.2 slice.3
  64.8 307.3 %conditional.1 = (bf16[128,4096]{1,0:T(8,128)(2,1)S(1)}) conditional(s32[]{:T(128)} %bitcast.2, (s32[128]{0:T(128)}, bf16[128,4096]{1,0:T(8,128)(2,1)}, bf16[128,512]{1,0:T(8,128)(2,1)}, bf16[128,512]{1,0:T(8,128)(2,1)}) %tuple.11, bf16[128,4096]{1,0:T(8,128)(2,1)S(1)} %get-tuple-element.27), branch_computations={%region_0.0_spmd, %region_1.0_spmd} | conditional | bytes 8 | solution.py:695
  64.9 67.0 %exchange.1 = (bf16[16,32,1024]{2,1,0:T(8,128)(2,1)}, bf16[32,1024,128]{2,1,0:T(8,128)(2,1)}, s32[8,128]{1,0:T(8,128)}) custom-call(s32[1,128]{1,0:T(1,128)} %bitcast.4, bf16[128,4096]{1,0:T(8,128)(2,1)} %get-tuple-element.18.q_in, bf16[128,512]{1,0:T(8,128)(2,1)} %get-tuple-element.19.k_in, bf16[128,512]{1,0:T(8,128)(2,1)} %get-tuple-element.20.v_in), custom_call_target="tpu_custom_call" | custom-call | tf_op jit(solution)/shard_map/cond/branch_0_fun/exchange/pallas_call | solution.py:377
  131.9 227.4 %attend.1.o_in = bf16[16,32,1024]{2,1,0:T(8,128)(2,1)} custom-call(s32[8,128]{1,0:T(8,128)} %get-tuple-element.21.info, bf16[16,32,1024]{2,1,0:T(8,128)(2,1)} %get-tuple-element.22.q_ref, bf16[32,1024,128]{2,1,0:T(8,128)(2,1)} %get-tuple-element.23.kv), custom_call_target="tpu_custom_call" | custom-call | tf_op jit(solution)/shard_map/cond/branch_0_fun/attend/pallas_call | solution.py:158
  359.3 12.8 %give_back.1 = bf16[128,4096]{1,0:T(8,128)(2,1)S(1)} custom-call(bf16[16,32,1024]{2,1,0:T(8,128)(2,1)} %attend.1.o_in), custom_call_target="tpu_custom_call" | custom-call | tf_op jit(solution)/shard_map/cond/branch_0_fun/give_back/pallas_call | solution.py:400
  372.1 1.0 copy.10

commit v5 on v4

--- a/solution.py
+++ b/solution.py
@@ -574,7 +574,7 @@
         start_later((x >= 2) & (y >= j), 7 + j, 8, 8 - j, peer("blk_1", RING - j))
     final = sum_stats(2)
     reach = final[NDOC:NDOC + 1] * final[NDOC + 1:NDOC + 2] * SCALE2 ** 2
-    stats_out[...] = jnp.broadcast_to(jnp.where(reach < LIMIT ** 2, 1, 0), stats_out.shape)
+    stats_out[0] = jnp.min(jnp.where(reach < LIMIT ** 2, 1, 0))
     starts = jnp.sum(final[:NDOC], axis=1, keepdims=True).astype(jnp.int32)
     starts = jnp.broadcast_to(starts, (NDOC, rows))
     own[2].wait()
@@ -666,10 +666,10 @@
         ring_attend,
         out_shape=(
             jax.ShapeDtypeStruct((rows, wide), jnp.bfloat16),
-            jax.ShapeDtypeStruct((8, rows), jnp.int32),
+            jax.ShapeDtypeStruct((1,), jnp.int32),
         ),
         in_specs=[vm, anywhere, anywhere, anywhere],
-        out_specs=(anywhere, vm),
+        out_specs=(anywhere, pl.BlockSpec(memory_space=pltpu.SMEM)),
         scratch_shapes=[
             pltpu.VMEM((2, (REACH + 1) * COLUMN, HEAD_SIZE), jnp.bfloat16),
             pltpu.VMEM((RING, rows, width), jnp.bfloat16),
@@ -692,7 +692,7 @@
         compiler_params=pltpu.CompilerParams(collective_id=0, has_side_effects=True, vmem_limit_bytes=56 << 20),
         name="ring_attend",
     )(segments.reshape(1, rows), queries, keys, values)
-    return lax.cond(stats[0, 0] == 1, lambda *_: out, careful, queries, keys, values, segments)
+    return lax.cond(stats[0] == 1, lambda *_: out, careful, queries, keys, values, segments)
 
 
 def solution(mesh):

time: 373 us -> 320 us (0.86)
  the two profiles are of different devices: /device:TPU:24 before, /device:TPU:31 now
where the time goes in v5:
time: 320 us; the launch traced here: 318 us
  Pallas kernels  316 us (99%)
    pallas_call x1, Pallas kernels, attention(): pl.pallas_call(functools.partial(attend, place), out_shape=jax.ShapeDtype...  176 us
    pallas_call x1, Pallas kernels, local(): pl.pallas_call(ring_attend, out_shape=(jax.ShapeDtypeStruct((rows, wide),...  68.8 us
    pallas_call x1, Pallas kernels, careful(): pl.pallas_call(exchange, out_shape=(jax.ShapeDtypeStruct((RING * RING, pi...  58.3 us
    pallas_call x1, Pallas kernels, careful(): pl.pallas_call(give_back, out_shape=jax.ShapeDtypeStruct((rows, wide), jn...  13.3 us

profile of v5, /device:TPU:31, one launch (start us, length us, event | category | flops | bytes accessed | tf_op | source)
XLA Modules:
  0.0 318.0 jit_solution(2663246151198624016)
XLA Ops:
  0.0 68.8 %ring_attend.1 = (bf16[128,4096]{1,0:T(8,128)(2,1)S(1)}, s32[1]{0:T(128)}) custom-call(s32[1,128]{1,0:T(1,128)} %bitcast.3, bf16[128,4096]{1,0:T(8,128)(2,1)} %q_in.1, bf16[128,512]{1,0:T(8,128)(2,1)} %k_in.1, bf16[128,512]{1,0:T(8,128)(2,1)} %v_in.1), custom_call_target="tpu_custom_call" | custom-call | tf_op jit(solution)/shard_map/ring_attend/pallas_call | solution.py:665
  69.4 247.7 %conditional.1 = (bf16[128,4096]{1,0:T(8,128)(2,1)S(1)}) conditional(s32[]{:T(128)} %bitcast.2, (s32[128]{0:T(128)}, bf16[128,4096]{1,0:T(8,128)(2,1)}, bf16[128,512]{1,0:T(8,128)(2,1)}, bf16[128,512]{1,0:T(8,128)(2,1)}) %tuple.11, bf16[128,4096]{1,0:T(8,128)(2,1)S(1)} %get-tuple-element.27), branch_computations={%region_0.0_spmd, %region_1.0_spmd} | conditional | bytes 8 | solution.py:695
  69.4 58.3 %exchange.1 = (bf16[16,32,1024]{2,1,0:T(8,128)(2,1)}, bf16[32,1024,128]{2,1,0:T(8,128)(2,1)}, s32[8,128]{1,0:T(8,128)}) custom-call(s32[1,128]{1,0:T(1,128)} %bitcast.4, bf16[128,4096]{1,0:T(8,128)(2,1)} %get-tuple-element.18.q_in, bf16[128,512]{1,0:T(8,128)(2,1)} %get-tuple-element.19.k_in, bf16[128,512]{1,0:T(8,128)(2,1)} %get-tuple-element.20.v_in), custom_call_target="tpu_custom_call" | custom-call | tf_op jit(solution)/shard_map/cond/branch_0_fun/exchange/pallas_call | solution.py:377
  127.7 176.0 %attend.1.o_in = bf16[16,32,1024]{2,1,0:T(8,128)(2,1)} custom-call(s32[8,128]{1,0:T(8,128)} %get-tuple-element.21.info, bf16[16,32,1024]{2,1,0:T(8,128)(2,1)} %get-tuple-element.22.q_ref, bf16[32,1024,128]{2,1,0:T(8,128)(2,1)} %get-tuple-element.23.kv), custom_call_target="tpu_custom_call" | custom-call | tf_op jit(solution)/shard_map/cond/branch_0_fun/attend/pallas_call | solution.py:158
  303.7 13.3 %give_back.1 = bf16[128,4096]{1,0:T(8,128)(2,1)S(1)} custom-call(bf16[16,32,1024]{2,1,0:T(8,128)(2,1)} %attend.1.o_in), custom_call_target="tpu_custom_call" | custom-call | tf_op jit(solution)/shard_map/cond/branch_0_fun/give_back/pallas_call | solution.py:400
  317.1 1.0 copy.10
